TPU v7x, 32 devices: a whole 2x2x4 slice. The times are simulated.
32 devices in a mesh: gx: 4 (over z), gy: 2 (over x), gz: 4 (over y, core).
Axes of the slice: x: 2, y: 2, z: 4, core: 2. Of those that a mesh axis runs over, the one named last changes fastest.
Arguments:
- snapshot: bfloat16 [16, 32, 96, 256], P(None, 'gx', 'gz', 'gy'), may hold values from -6 to 6
- factor_two: bfloat16 [256, 128], P('gy'), may hold values from -0.375 to 0.375
- factor_three: bfloat16 [96, 48], P('gz'), may hold values from -0.625 to 0.625
Outputs:
- gram: float32 [32, 32], P('gx', ('gy', 'gz'))
All inputs are finite; a program needn't handle non-finite values.
Results may differ from a plain program's by a relative error of at most 0.0003.
Values may be sent and summed in bfloat16 or wider, within the bound.
A program may use at most 64 MiB of HBM per device.

v0:
```python
import jax
import jax.numpy as jnp
from jax import lax
from jax.sharding import PartitionSpec as P

S = 16
R2 = 128
R3 = 48


def per_device(snapshot, factor_two, factor_three):
    columns = factor_three
    third_share = lax.psum_scatter(
        jnp.einsum("sikj,kr->rsij", snapshot, columns, preferred_element_type=jnp.float32),
        "gz",
        scatter_dimension=0,
        tiled=True,
    )
    columns = factor_two.astype(jnp.float32)
    second_share = lax.psum_scatter(
        jnp.einsum("rsij,jq->qrsi", third_share, columns, precision=lax.Precision.HIGHEST),
        "gy",
        scatter_dimension=0,
        tiled=True,
    ).astype(jnp.bfloat16)
    fibres = second_share.reshape((-1, second_share.shape[3]))
    regrouped = lax.all_to_all(fibres, "gx", split_axis=0, concat_axis=1, tiled=True)
    partial_gram = lax.psum_scatter(
        jnp.dot(regrouped.T, regrouped, preferred_element_type=jnp.float32),
        "gx",
        scatter_dimension=0,
        tiled=True,
    )
    summed = lax.psum_scatter(partial_gram, ("gy", "gz"), scatter_dimension=1, tiled=True)
    return summed / float(R2 * R3 * S)


def solution(mesh):
    placed = (P(None, "gx", "gz", "gy"), P("gy", None), P("gz", None))
    return jax.shard_map(
        per_device, mesh=mesh, in_specs=placed, out_specs=P("gx", ("gy", "gz")), check_vma=False
    )
```

profile of v0, /device:TPU:0, one launch (start us, length us, event | category | flops | bytes accessed | tf_op | source)
XLA Modules:
  0.0 126.5 jit_solution(10171021634183022220)
XLA Ops:
  6.5 0.0 copy-start
  6.5 0.0 reduce-scatter.6.cloned.1.call-start
  6.5 1.1 copy-done
  7.7 1.3 %fusion.4 = f32[48,16,8,128]{3,0,2,1:T(8,128)S(1)} fusion(bf16[16,8,24,128]{3,2,1,0:T(8,128)(2,1)S(1)} %copy-done, bf16[24,48]{1,0:T(8,128)(2,1)} %param.5), kind=kOutput, calls=%fused_computation.4 | convolution fusion | flops 37748736 | bytes 3934464 | tf_op jit(solution)/shard_map/sikj,kr->rsij/dot_general | solution.py:14
  9.0 2.6 %copy.12 = f32[48,16,8,128]{3,2,1,0:T(8,128)} copy(f32[48,16,8,128]{3,0,2,1:T(8,128)S(1)} %fusion.4) | data formatting | bytes 6291456 | tf_op jit(solution)/shard_map/sikj,kr->rsij/dot_general | solution.py:14
  11.6 0.0 copy-start.1
  11.6 0.0 reduce-scatter.6.cloned.1.call-update
  11.6 0.0 reduce-scatter.8.cloned.1.call-start
  11.7 40.8 %reduce-scatter.6.cloned.1.call-done = f32[12,16,8,128]{3,2,1,0:T(8,128)} async-done(((f32[48,16,8,128]{3,2,1,0:T(8,128)}), f32[12,16,8,128]{3,2,1,0:T(8,128)}) %reduce-scatter.6.cloned.1.call-update) | async-done | bytes 786448 | tf_op jit(solution)/shard_map/reduce_scatter | solution.py:13
  52.4 0.0 copy-done.1
  52.4 1.6 %fusion.2 = f32[12,16,8,128]{3,2,1,0:T(8,128)S(1)} fusion(f32[12,16,8,128]{3,2,1,0:T(8,128)} %reduce-scatter.6.cloned.1.call-done, bf16[128,128]{1,0:T(8,128)(2,1)S(1)} %copy-done.1), kind=kOutput, calls=%fused_computation.2 | convolution fusion | flops 301989888 | bytes 1605632 | tf_op jit(solution)/shard_map/rsij,jq->qrsi/dot_general | solution.py:21
  54.0 1.2 copy.21
  55.2 0.0 reduce-scatter.8.cloned.1.call-update
  55.2 0.0 copy-start.3
  55.2 0.0 copy-start.2
  55.2 17.6 %reduce-scatter.8.cloned.1.call-done = f32[64,1536]{1,0:T(8,128)} async-done(((f32[128,1536]{1,0:T(8,128)}), f32[64,1536]{1,0:T(8,128)}) %reduce-scatter.8.cloned.1.call-update) | async-done | bytes 393232
  72.8 1.2 copy.22
  74.0 1.5 %copy.13 = bf16[64,12,16,8]{2,1,0,3:T(8,128)(2,1)S(1)} copy(bf16[64,12,16,8]{0,3,2,1:T(8,128)(2,1)S(1)} %bitcast.29) | data formatting | bytes 393216 | tf_op jit(solution)/shard_map/convert_element_type | solution.py:25
  75.6 1.7 %all_to_all.14 = bf16[4,3072,8]{1,0,2:T(4,128)(2,1)S(1)} reshape(bf16[64,12,16,8]{2,1,0,3:T(8,128)(2,1)S(1)} %copy.13) | data formatting | bytes 393216 | tf_op jit(solution)/shard_map/all_to_all | solution.py:27
  77.3 0.7 copy.14
  78.0 4.6 %all-to-all-start = ((bf16[4,3072,8]{1,2,0:T(8,128)(2,1)}), bf16[4,3072,8]{1,2,0:T(8,128)(2,1)S(1)}, u32[]{:S(2)}, u32[]{:S(2)}) async-start(bf16[4,3072,8]{1,2,0:T(8,128)(2,1)} %copy.14), calls=%async_computation.1 | async-start | bytes 393216 | tf_op jit(solution)/shard_map/all_to_all | solution.py:27
  82.6 0.0 copy-done.3
  82.6 0.6 dynamic-slice
  83.2 0.0 copy-done.2
  83.2 0.6 dynamic-slice.2
  85.1 5.0 %all-to-all-done = bf16[4,3072,8]{1,2,0:T(8,128)(2,1)S(1)} async-done(((bf16[4,3072,8]{1,2,0:T(8,128)(2,1)}), bf16[4,3072,8]{1,2,0:T(8,128)(2,1)S(1)}, u32[]{:S(2)}, u32[]{:S(2)}) %all-to-all-start) | async-done | bytes 196640 | tf_op jit(solution)/shard_map/all_to_all | solution.py:27
  90.1 0.2 fusion
  90.3 16.8 %all-reduce = f32[32,32]{1,0:T(8,128)S(1)} all-reduce(f32[32,32]{1,0:T(8,128)S(1)} %fusion), channel_id=4, replica_groups=mesh['gx'=4,'gy'=2,'gz'=4] {'gx'}, use_global_device_ids=true, to_apply=%region_2.0.clone | all-reduce | flops 1024 | bytes 8192
  107.1 11.8 %all-reduce.1 = f32[8,32]{1,0:T(8,128)S(1)} all-reduce(f32[8,32]{1,0:T(8,128)S(1)} %constant_dynamic-slice_fusion), channel_id=5, replica_groups=mesh['gx'=4,'gy'=2,'gz'=4] {'gy','gz'}, use_global_device_ids=true, to_apply=%region_3.0.clone | all-reduce | flops 256 | bytes 2048
  118.9 0.1 dynamic-slice_multiply_fusion
  119.0 0.7 copy.15
  (1 shorter events, 0.0 us)
Async XLA Ops:
  6.5 1.1 copy-start
  6.5 45.9 %reduce-scatter.6.cloned.1.call-start = ((), (), s32[]{:S(2)}) async-start(), calls=%async_computation.3 | async-start | bytes 3932160 | tf_op jit(solution)/shard_map/reduce_scatter | solution.py:13
  11.6 40.8 %copy-start.1 = (bf16[128,128]{1,0:T(8,128)(2,1)S(1)}, bf16[128,128]{1,0:T(8,128)(2,1)}, u32[]{:S(2)}) copy-start(bf16[128,128]{1,0:T(8,128)(2,1)} %param.4) | copy-start | bytes 98308
  11.6 61.2 %reduce-scatter.8.cloned.1.call-start = ((), (), s32[]{:S(2)}) async-start(), calls=%async_computation.4 | async-start | bytes 1179648
  55.2 27.4 %copy-start.3 = (u32[32]{0:T(128)S(1)}, u32[32]{0:T(128)}, u32[]{:S(2)}) copy-start(u32[32]{0:T(128)} %constant.5) | copy-start | bytes 388
  55.2 28.0 %copy-start.2 = (u32[32]{0:T(128)S(1)}, u32[32]{0:T(128)}, u32[]{:S(2)}) copy-start(u32[32]{0:T(128)} %constant.9) | copy-start | bytes 388
  78.0 12.1 %all-to-all-start = ((bf16[4,3072,8]{1,2,0:T(8,128)(2,1)}), bf16[4,3072,8]{1,2,0:T(8,128)(2,1)S(1)}, u32[]{:S(2)}, u32[]{:S(2)}) async-start(bf16[4,3072,8]{1,2,0:T(8,128)(2,1)} %copy.14), calls=%async_computation.1 | async-start | bytes 393216 | tf_op jit(solution)/shard_map/all_to_all | solution.py:27
Sparse Core Ops, SparseCore 0:
  11.7 40.6 reduce-scatter.5
  55.3 17.4 reduce-scatter.7
where the time goes:
time: 127 us; the launch traced here: 126 us
  waiting for transfers between devices  63.4 us (50%)
  blocking collectives  28.6 us (23%)
  between operations  14.7 us (12%)
  local copies, waits for them, and re-layouts  12 us (9%)
  starting transfers between devices  4.63 us (4%)
  matrix products  3.06 us (2%)
    reduce_scatter x1, waiting for transfers between devices, per_device(): lax.psum_scatter(jnp.einsum('sikj,kr->rsij', snapshot, columns, preferred...  40.8 us
    unnamed x2, blocking collectives  28.6 us
    unnamed x3, waiting for transfers between devices  17.6 us
    all_to_all x1, waiting for transfers between devices, per_device(): lax.all_to_all(fibres, 'gx', split_axis=0, concat_axis=1, tiled=True)  5.03 us
    unnamed x13, local copies, waits for them, and re-layouts  4.71 us
    all_to_all x1, starting transfers between devices, per_device(): lax.all_to_all(fibres, 'gx', split_axis=0, concat_axis=1, tiled=True)  4.58 us
    dot_general x1, local copies, waits for them, and re-layouts, per_device(): jnp.einsum('sikj,kr->rsij', snapshot, columns, preferred_element_type=jnp...  2.63 us
  transfers between devices with their start and end apart: 3, of which 3 were waited for; matrix products, arithmetic and copies ran while one was open for 1% of the time, Pallas kernels for 0%

commit v1 on v0

v1 whole, which is shorter than its diff:
```python
import functools

import jax
import jax.numpy as jnp
from jax import lax
from jax.experimental import pallas as pl
from jax.experimental.pallas import tpu as pltpu
from jax.sharding import PartitionSpec as P

MESH = pl.DeviceIdType.MESH
NT = (((1,), (1,)), ((), ()))


def kernel(dims, snap, f2, f3, out, rx, f2rx, f3own, f3rx, mix, z32, tx2, rx2, g, rx3, h, rx4,
           local_sem, send1, recv1, sendf2, recvf2, sendf3, recvf3, send2, recv2, send3, recv3, send4, recv4):
    GX, GY, GZ, S, C, H, NI, K, R3, N1, total = dims
    G = GY * GZ
    x, y, z = lax.axis_index("gx"), lax.axis_index("gy"), lax.axis_index("gz")
    me = y * GZ + z

    def plane(p):
        return {"gy": lax.div(p, GZ), "gz": lax.rem(p, GZ)}

    def plus(index, offset, size):
        return lax.rem(index + offset, size)

    def species(p, c):
        return lax.div(p, H) * C + c

    def remote(src, dst, send, recv, device):
        return pltpu.make_async_remote_copy(
            src_ref=src, dst_ref=dst, send_sem=send, recv_sem=recv, device_id=device, device_id_type=MESH)

    barrier = pltpu.get_barrier_semaphore()
    for o in range(1, G):
        pl.semaphore_signal(barrier, inc=1, device_id=plane(plus(me, o, G)), device_id_type=MESH)
    for o in range(1, GX):
        pl.semaphore_signal(barrier, inc=1, device_id={"gx": plus(x, o, GX)}, device_id_type=MESH)
    f3own[...] = f3[...].astype(jnp.float32)
    f3rx[z] = f3own[...]
    g[...] = jnp.zeros_like(g)
    own = [pltpu.make_async_copy(snap.at[species(me, c)], rx.at[c, me], local_sem.at[c]) for c in range(C)]
    own.append(pltpu.make_async_copy(f2, f2rx.at[y], local_sem.at[C]))
    for copy in own:
        copy.start()
    pl.semaphore_wait(barrier, G - 1 + GX - 1)

    sends = []
    for o in range(1, GY):
        sends.append(remote(f2, f2rx.at[y], sendf2.at[o], recvf2.at[o], {"gy": plus(y, o, GY)}))
    for o in range(1, GZ):
        sends.append(remote(f3own, f3rx.at[z], sendf3.at[o], recvf3.at[o], {"gz": plus(z, o, GZ)}))
    for c in range(C):
        for o in range(1, G):
            p = plus(me, o, G)
            sends.append(remote(snap.at[species(p, c)], rx.at[c, me], send1.at[c, o], recv1.at[c, o], plane(p)))
    for copy in sends:
        copy.start()

    for o in range(1, GY):
        q = plus(y, GY - o, GY)
        remote(f2, f2rx.at[q], sendf2.at[o], recvf2.at[o], {"gy": q}).wait_recv()
    own[C].wait()
    for o in range(1, GZ):
        q = plus(z, GZ - o, GZ)
        remote(f3own, f3rx.at[q], sendf3.at[o], recvf3.at[o], {"gz": q}).wait_recv()
    whole2 = jnp.concatenate([f2rx[b] for b in range(GY)], axis=0)
    if H > 1:
        R2 = whole2.shape[1]
        lanes = lax.div(lax.broadcasted_iota(jnp.int32, whole2.shape, 1), R2 // H)
        whole2 = jnp.where(lanes == lax.rem(me, H), whole2.astype(jnp.float32), 0.0).astype(jnp.bfloat16)
    whole3 = jnp.concatenate([f3rx[b] for b in range(GZ)] * 2, axis=0).astype(jnp.bfloat16)
    rows = lax.broadcasted_iota(jnp.int32, (R3, R3), 0)
    cols = lax.broadcasted_iota(jnp.int32, (R3, R3), 1)
    unit = jnp.where(rows == cols, 1.0, 0.0).astype(jnp.bfloat16)
    mix[...] = lax.dot_general(unit, whole3, NT, preferred_element_type=jnp.float32).astype(jnp.bfloat16)

    for c in range(C):
        own[c].wait()
        for o in range(1, G):
            p = plus(me, G - o, G)
            remote(snap.at[0], rx.at[c, p], send1.at[c, o], recv1.at[c, o], plane(p)).wait_recv()
        second = []
        for b in range(GZ):
            cells = jnp.concatenate([rx[c, a * GZ + b] for a in range(GY)], axis=1)
            second.append(jnp.dot(cells, whole2, preferred_element_type=jnp.float32))
        for i in range(0, NI, 2):
            pair = []
            for n in (i, i + 1):
                fibre = jnp.concatenate([block[n * K:(n + 1) * K] for block in second], axis=0)
                high = fibre.astype(jnp.bfloat16)
                low = (fibre - high.astype(jnp.float32)).astype(jnp.bfloat16)
                pair.append(jnp.concatenate([high, low], axis=0))
            both = jnp.dot(mix[...], jnp.concatenate(pair, axis=1), preferred_element_type=jnp.float32)
            R2 = both.shape[1] // 2
            z32[c, pl.ds(i, R3, stride=NI), :] = both[:, :R2]
            z32[c, pl.ds(i + 1, R3, stride=NI), :] = both[:, R2:]
        share = R3 // GX * NI
        for b in range(GX):
            tx2[c, b] = z32[c, b * share:(b + 1) * share, :].astype(jnp.bfloat16)
        for o in range(1, GX):
            q = plus(x, o, GX)
            copy = remote(tx2.at[c, q], rx2.at[c, x], send2.at[c, o], recv2.at[c, o], {"gx": q})
            copy.start()
            sends.append(copy)
        rx2[c, x] = tx2[c, x]

    gram = None
    for c in range(C):
        for o in range(1, GX):
            q = plus(x, GX - o, GX)
            remote(tx2.at[c, q], rx2.at[c, q], send2.at[c, o], recv2.at[c, o], {"gx": q}).wait_recv()
        blocks = [rx2[c, b].astype(jnp.float32) for b in range(GX)]
        fibres = jnp.concatenate(
            [jnp.concatenate([block[r * NI:(r + 1) * NI] for block in blocks], axis=0) for r in range(R3 // GX)],
            axis=1).astype(jnp.bfloat16)
        term = lax.dot_general(fibres, fibres, NT, preferred_element_type=jnp.float32)
        gram = term if gram is None else gram + term

    for b in range(GX):
        g[b, :, :N1] = gram[b * NI:(b + 1) * NI]
    for o in range(1, GX):
        q = plus(x, o, GX)
        copy = remote(g.at[q], rx3.at[x], send3.at[o], recv3.at[o], {"gx": q})
        copy.start()
        sends.append(copy)
    rx3[x] = g[x]
    for o in range(1, GX):
        q = plus(x, GX - o, GX)
        remote(g.at[q], rx3.at[q], send3.at[o], recv3.at[o], {"gx": q}).wait_recv()
    h[...] = jnp.sum(rx3[...], axis=0)
    for o in range(1, G):
        copy = remote(h, rx4.at[me], send4.at[o], recv4.at[o], plane(plus(me, o, G)))
        copy.start()
        sends.append(copy)
    rx4[me] = h[...]
    for o in range(1, G):
        p = plus(me, G - o, G)
        remote(h, rx4.at[p], send4.at[o], recv4.at[o], plane(p)).wait_recv()
    summed = jnp.sum(rx4[...], axis=0)
    width = out.shape[1]
    lanes = summed.shape[1]
    summed = pltpu.roll(summed, lax.rem(lanes - width * me, lanes), 1)
    out[...] = summed[:, :width] / total
    for copy in sends:
        copy.wait_send()


def solution(mesh):
    GX, GY, GZ = (mesh.shape[name] for name in ("gx", "gy", "gz"))
    G = GY * GZ

    def per_device(snapshot, factor_two, factor_three):
        S, NI, K, J = snapshot.shape
        R2, R3 = factor_two.shape[1], factor_three.shape[1]
        N1 = NI * GX
        C, H = max(1, S // G), max(1, G // S)
        share = R3 // GX * NI
        lanes = -(-N1 // 128) * 128
        dims = (GX, GY, GZ, S, C, H, NI, K, R3, N1, float(R2 * R3 * S))
        dma = pltpu.SemaphoreType.DMA
        f32, bf16 = jnp.float32, jnp.bfloat16
        return pl.pallas_call(
            functools.partial(kernel, dims),
            out_shape=jax.ShapeDtypeStruct((NI, N1 // G), f32),
            in_specs=[pl.BlockSpec(memory_space=pl.ANY), pl.BlockSpec(memory_space=pl.ANY),
                      pl.BlockSpec(memory_space=pltpu.VMEM)],
            out_specs=pl.BlockSpec(memory_space=pltpu.VMEM),
            scratch_shapes=[
                pltpu.VMEM((C, G, NI * K, J), bf16),
                pltpu.VMEM((GY, J, R2), bf16),
                pltpu.VMEM((K, R3), f32),
                pltpu.VMEM((GZ, K, R3), f32),
                pltpu.VMEM((R3, 2 * GZ * K), bf16),
                pltpu.VMEM((C, R3 * NI, R2), f32),
                pltpu.VMEM((C, GX, share, R2), bf16),
                pltpu.VMEM((C, GX, share, R2), bf16),
                pltpu.VMEM((GX, NI, lanes), f32),
                pltpu.VMEM((GX, NI, lanes), f32),
                pltpu.VMEM((NI, lanes), f32),
                pltpu.VMEM((G, NI, lanes), f32),
                dma((C + 1,)),
                dma((C, G)), dma((C, G)),
                dma((GY,)), dma((GY,)),
                dma((GZ,)), dma((GZ,)),
                dma((C, GX)), dma((C, GX)),
                dma((GX,)), dma((GX,)),
                dma((G,)), dma((G,)),
            ],
            compiler_params=pltpu.CompilerParams(
                collective_id=0, has_side_effects=True, vmem_limit_bytes=32 * 1024 * 1024),
        )(snapshot.reshape(S, NI * K, J), factor_two, factor_three)

    placed = (P(None, "gx", "gz", "gy"), P("gy", None), P("gz", None))
    return jax.shard_map(
        per_device, mesh=mesh, in_specs=placed, out_specs=P("gx", ("gy", "gz")), check_vma=False
    )
```

time: 127 us -> 32.2 us (0.25)
  waiting for transfers between devices: 63.4 us -> 0 us
  Pallas kernels: 0 us -> 28.7 us
  blocking collectives: 28.6 us -> 0 us
  between operations: 14.7 us -> 0.01 us
  local copies, waits for them, and re-layouts: 12 us -> 3.23 us
  starting transfers between devices: 4.63 us -> 0 us
  matrix products: 3.06 us -> 0 us
    reduce_scatter x1 -> x0, waiting for transfers between devices: 40.8 us -> none  [per_device(): lax.psum_scatter(jnp.einsum('sikj,kr->rsij', snapshot, columns, preferred...]
    pallas_call x0 -> x1, Pallas kernels: none -> 28.7 us  [per_device(): pl.pallas_call(functools.partial(kernel, dims), out_shape=jax.ShapeDtypeS...]
    unnamed x2 -> x0, blocking collectives: 28.6 us -> none
    unnamed x3 -> x0, waiting for transfers between devices: 17.6 us -> none
    all_to_all x1 -> x0, waiting for transfers between devices: 5.03 us -> none  [per_device(): lax.all_to_all(fibres, 'gx', split_axis=0, concat_axis=1, tiled=True)]
    all_to_all x1 -> x0, starting transfers between devices: 4.58 us -> none  [per_device(): lax.all_to_all(fibres, 'gx', split_axis=0, concat_axis=1, tiled=True)]
    dot_general x3 -> x0, matrix products: 3.06 us -> none  [the longest x1 1.61 us: per_device(): jnp.einsum('rsij,jq->qrsi', third_share, columns, precision=lax.Precision...]
    dot_general x1 -> x0, local copies, waits for them, and re-layouts: 2.63 us -> none  [per_device(): jnp.einsum('sikj,kr->rsij', snapshot, columns, preferred_element_type=jnp...]
  transfers between devices with their start and end apart: 3 -> 0, of which waited for: 3 -> 0; matrix products, arithmetic and copies ran while one was open for 1% -> 0% of each run, Pallas kernels for 0% -> 0%
where the time goes in v1:
time: 32.2 us; the launch traced here: 31.9 us
  Pallas kernels  28.7 us (89%)
  local copies, waits for them, and re-layouts  3.23 us (10%)
    pallas_call x1, Pallas kernels, per_device(): pl.pallas_call(functools.partial(kernel, dims), out_shape=jax.ShapeDtypeS...  28.7 us
    unnamed x6, local copies, waits for them, and re-layouts  2.58 us
    pallas_call x1, local copies, waits for them, and re-layouts, per_device(): pl.pallas_call(functools.partial(kernel, dims), out_shape=jax.ShapeDtypeS...  0.65 us

profile of v1, /device:TPU:0, one launch (start us, length us, event | category | flops | bytes accessed | tf_op | source)
XLA Modules:
  0.0 31.9 jit_solution(16636200697735525315)
XLA Ops:
  0.0 0.0 copy-start
  0.0 1.1 %copy-done = bf16[16,8,24,128]{3,2,1,0:T(8,128)(2,1)S(1)} copy-done((bf16[16,8,24,128]{3,2,1,0:T(8,128)(2,1)S(1)}, bf16[16,8,24,128]{3,2,1,0:T(8,128)(2,1)}, u32[]{:S(2)}) %copy-start) | copy-done | bytes 786456
  1.1 0.0 copy-start.1
  1.1 0.8 %copy-done.1 = bf16[128,128]{1,0:T(8,128)(2,1)S(1)} copy-done((bf16[128,128]{1,0:T(8,128)(2,1)S(1)}, bf16[128,128]{1,0:T(8,128)(2,1)}, u32[]{:S(2)}) %copy-start.1) | copy-done | bytes 32792
  1.9 0.0 copy-start.2
  1.9 0.7 %copy-done.2 = bf16[24,48]{1,0:T(8,128)(2,1)S(1)} copy-done((bf16[24,48]{1,0:T(8,128)(2,1)S(1)}, bf16[24,48]{1,0:T(8,128)(2,1)}, u32[]{:S(2)}) %copy-start.2) | copy-done | bytes 2328
  2.6 28.7 %shard_map.37 = f32[8,4]{1,0:T(8,128)S(1)} custom-call(bf16[16,192,128]{2,1,0:T(8,128)(2,1)S(1)} %bitcast.1, bf16[128,128]{1,0:T(8,128)(2,1)S(1)} %copy-done.1, bf16[24,48]{1,0:T(8,128)(2,1)S(1)} %copy-done.2), custom_call_target="tpu_custom_call" | custom-call | tf_op jit(solution)/shard_map/pallas_call | solution.py:163
  31.3 0.7 %copy.4 = f32[8,4]{0,1:T(4,128)} copy(f32[8,4]{1,0:T(8,128)S(1)} %shard_map.37) | data formatting | bytes 256 | tf_op jit(solution)/shard_map/pallas_call | solution.py:163
Async XLA Ops:
  0.0 1.1 %copy-start = (bf16[16,8,24,128]{3,2,1,0:T(8,128)(2,1)S(1)}, bf16[16,8,24,128]{3,2,1,0:T(8,128)(2,1)}, u32[]{:S(2)}) copy-start(bf16[16,8,24,128]{3,2,1,0:T(8,128)(2,1)} %param.3) | copy-start | bytes 2359300
  1.1 0.8 %copy-start.1 = (bf16[128,128]{1,0:T(8,128)(2,1)S(1)}, bf16[128,128]{1,0:T(8,128)(2,1)}, u32[]{:S(2)}) copy-start(bf16[128,128]{1,0:T(8,128)(2,1)} %f2.1) | copy-start | bytes 98308
  1.9 0.7 %copy-start.2 = (bf16[24,48]{1,0:T(8,128)(2,1)S(1)}, bf16[24,48]{1,0:T(8,128)(2,1)}, u32[]{:S(2)}) copy-start(bf16[24,48]{1,0:T(8,128)(2,1)} %f3.1) | copy-start | bytes 6916

commit v2 on v1

v2 whole, which is shorter than its diff:
```python
import functools

import jax
import jax.numpy as jnp
from jax import lax
from jax.experimental import pallas as pl
from jax.experimental.pallas import tpu as pltpu
from jax.sharding import PartitionSpec as P

MESH = pl.DeviceIdType.MESH
NT = (((1,), (1,)), ((), ()))


def kernel(dims, snap, f2, f3, out, rx, f2rx, f3raw, f3own, f3rx, mix, z32, tx2, rx2, g, rx4,
           local_sem, send1, recv1, sendf2, recvf2, sendf3, recvf3, send2, recv2, send4, recv4, line):
    GX, GY, GZ, S, C, D, H, NI, K, R3, N1, total = dims
    G = GY * GZ
    T, NI_, W = C * D, NI // D, N1 // G
    x, y, z = lax.axis_index("gx"), lax.axis_index("gy"), lax.axis_index("gz")
    me = y * GZ + z

    def plane(p):
        return {"gy": lax.div(p, GZ), "gz": lax.rem(p, GZ)}

    def plus(index, offset, size):
        return lax.rem(index + offset, size)

    def cells(p, t):
        return snap.at[lax.div(p, H) * C + t // D, pl.ds(t % D * NI_ * K, NI_ * K)]

    def remote(src, dst, send, recv, device):
        return pltpu.make_async_remote_copy(
            src_ref=src, dst_ref=dst, send_sem=send, recv_sem=recv, device_id=device, device_id_type=MESH)

    barrier = pltpu.get_barrier_semaphore()
    for o in range(1, G):
        pl.semaphore_signal(barrier, inc=1, device_id=plane(plus(me, o, G)), device_id_type=MESH)
    def neighbours(semaphore):
        @pl.when(x > 0)
        def _():
            pl.semaphore_signal(semaphore, inc=1, device_id={"gx": x - 1}, device_id_type=MESH)

        @pl.when(x < GX - 1)
        def _():
            pl.semaphore_signal(semaphore, inc=1, device_id={"gx": x + 1}, device_id_type=MESH)

    beside = jnp.where(x > 0, 1, 0) + jnp.where(x < GX - 1, 1, 0)
    neighbours(barrier)
    first = pltpu.make_async_copy(f3, f3raw, local_sem.at[T + 1])
    first.start()
    own = [pltpu.make_async_copy(cells(me, t), rx.at[t, me], local_sem.at[t]) for t in range(T)]
    own.append(pltpu.make_async_copy(f2, f2rx.at[y], local_sem.at[T]))
    for copy in own:
        copy.start()
    first.wait()
    f3own[...] = f3raw[...].astype(jnp.float32)
    f3rx[z] = f3own[...]
    g[...] = jnp.zeros_like(g)
    pl.semaphore_wait(barrier, G - 1 + beside)

    sends = []
    for o in range(1, GY):
        sends.append(remote(f2, f2rx.at[y], sendf2.at[o], recvf2.at[o], {"gy": plus(y, o, GY)}))
    for o in range(1, GZ):
        sends.append(remote(f3own, f3rx.at[z], sendf3.at[o], recvf3.at[o], {"gz": plus(z, o, GZ)}))
    for t in range(T):
        for o in range(1, G):
            p = plus(me, o, G)
            sends.append(remote(cells(p, t), rx.at[t, me], send1.at[t, o], recv1.at[t, o], plane(p)))
    for copy in sends:
        copy.start()

    for step in range(GX - 2):
        neighbours(line.at[step])
        pl.semaphore_wait(line.at[step], beside)

    for o in range(1, GY):
        q = plus(y, GY - o, GY)
        remote(f2, f2rx.at[q], sendf2.at[o], recvf2.at[o], {"gy": q}).wait_recv()
    own[T].wait()
    for o in range(1, GZ):
        q = plus(z, GZ - o, GZ)
        remote(f3own, f3rx.at[q], sendf3.at[o], recvf3.at[o], {"gz": q}).wait_recv()
    whole2 = jnp.concatenate([f2rx[b] for b in range(GY)], axis=0)
    if H > 1:
        R2 = whole2.shape[1]
        lanes = lax.div(lax.broadcasted_iota(jnp.int32, whole2.shape, 1), R2 // H)
        whole2 = jnp.where(lanes == lax.rem(me, H), whole2.astype(jnp.float32), 0.0).astype(jnp.bfloat16)
    whole3 = jnp.concatenate([f3rx[b] for b in range(GZ)] * 2, axis=0).astype(jnp.bfloat16)
    rows = lax.broadcasted_iota(jnp.int32, (R3, R3), 0)
    cols = lax.broadcasted_iota(jnp.int32, (R3, R3), 1)
    unit = jnp.where(rows == cols, 1.0, 0.0).astype(jnp.bfloat16)
    mix[...] = lax.dot_general(unit, whole3, NT, preferred_element_type=jnp.float32).astype(jnp.bfloat16)

    for t in range(T):
        own[t].wait()
        for o in range(1, G):
            p = plus(me, G - o, G)
            remote(cells(me, t), rx.at[t, p], send1.at[t, o], recv1.at[t, o], plane(p)).wait_recv()
        second = []
        for b in range(GZ):
            wide = jnp.concatenate([rx[t, a * GZ + b] for a in range(GY)], axis=1)
            second.append(jnp.dot(wide, whole2, preferred_element_type=jnp.float32))
        for i in range(0, NI_, 2):
            pair = []
            for n in (i, i + 1):
                fibre = jnp.concatenate([block[n * K:(n + 1) * K] for block in second], axis=0)
                high = fibre.astype(jnp.bfloat16)
                low = (fibre - high.astype(jnp.float32)).astype(jnp.bfloat16)
                pair.append(jnp.concatenate([high, low], axis=0))
            both = jnp.dot(mix[...], jnp.concatenate(pair, axis=1), preferred_element_type=jnp.float32)
            R2 = both.shape[1] // 2
            z32[t, pl.ds(i, R3, stride=NI_), :] = both[:, :R2]
            z32[t, pl.ds(i + 1, R3, stride=NI_), :] = both[:, R2:]
        share = R3 // GX * NI_
        for b in range(GX):
            tx2[t, b] = z32[t, b * share:(b + 1) * share, :].astype(jnp.bfloat16)
        for o in range(1, GX):
            q = plus(x, o, GX)
            copy = remote(tx2.at[t, q], rx2.at[t, x], send2.at[t, o], recv2.at[t, o], {"gx": q})
            copy.start()
            sends.append(copy)
        rx2[t, x] = tx2[t, x]

    gram = None
    for c in range(C):
        for t in range(c * D, c * D + D):
            for o in range(1, GX):
                q = plus(x, GX - o, GX)
                remote(tx2.at[t, q], rx2.at[t, q], send2.at[t, o], recv2.at[t, o], {"gx": q}).wait_recv()
        blocks = [rx2[c * D + d, b].astype(jnp.float32) for b in range(GX) for d in range(D)]
        fibres = jnp.concatenate(
            [jnp.concatenate([block[r * NI_:(r + 1) * NI_] for block in blocks], axis=0) for r in range(R3 // GX)],
            axis=1).astype(jnp.bfloat16)
        term = lax.dot_general(fibres, fibres, NT, preferred_element_type=jnp.float32)
        gram = term if gram is None else gram + term

    for b in range(G):
        g[b, :, :N1] = gram[b * W:(b + 1) * W]
    flat, N = x * G + me, GX * G
    for o in range(1, N):
        d = lax.rem(flat + o, N)
        dx, dp = lax.div(d, G), lax.rem(d, G)
        copy = remote(g.at[dp], rx4.at[flat], send4.at[o], recv4.at[o], {"gx": dx, **plane(dp)})
        copy.start()
        sends.append(copy)
    rx4[flat] = g[me]
    for o in range(1, N):
        d = lax.rem(flat + N - o, N)
        remote(g.at[0], rx4.at[d], send4.at[o], recv4.at[o], {"gx": lax.div(d, G), **plane(lax.rem(d, G))}).wait_recv()
    summed = jnp.sum(rx4[...], axis=0)
    lanes = summed.shape[1]
    summed = pltpu.roll(summed, lax.rem(lanes - NI * x, lanes), 1)
    out[...] = summed[:, :NI] / total
    for copy in sends:
        copy.wait_send()


def solution(mesh):
    GX, GY, GZ = (mesh.shape[name] for name in ("gx", "gy", "gz"))
    G = GY * GZ

    def per_device(snapshot, factor_two, factor_three):
        S, NI, K, J = snapshot.shape
        R2, R3 = factor_two.shape[1], factor_three.shape[1]
        N1 = NI * GX
        C, H = max(1, S // G), max(1, G // S)
        share = R3 // GX * NI
        lanes = -(-N1 // 128) * 128
        D = 2 if share % 32 == 0 else 1
        part = NI // D
        dims = (GX, GY, GZ, S, C, D, H, NI, K, R3, N1, float(R2 * R3 * S))
        dma = pltpu.SemaphoreType.DMA
        f32, bf16 = jnp.float32, jnp.bfloat16
        return pl.pallas_call(
            functools.partial(kernel, dims),
            out_shape=jax.ShapeDtypeStruct((N1 // G, NI), f32),
            in_specs=[pl.BlockSpec(memory_space=pl.ANY)] * 3,
            out_specs=pl.BlockSpec(memory_space=pltpu.VMEM),
            scratch_shapes=[
                pltpu.VMEM((C * D, G, part * K, J), bf16),
                pltpu.VMEM((GY, J, R2), bf16),
                pltpu.VMEM((K, R3), bf16),
                pltpu.VMEM((K, R3), f32),
                pltpu.VMEM((GZ, K, R3), f32),
                pltpu.VMEM((R3, 2 * GZ * K), bf16),
                pltpu.VMEM((C * D, R3 * part, R2), f32),
                pltpu.VMEM((C * D, GX, share // D, R2), bf16),
                pltpu.VMEM((C * D, GX, share // D, R2), bf16),
                pltpu.VMEM((G, N1 // G, lanes), f32),
                pltpu.VMEM((GX * G, N1 // G, lanes), f32),
                dma((C * D + 2,)),
                dma((C * D, G)), dma((C * D, G)),
                dma((GY,)), dma((GY,)),
                dma((GZ,)), dma((GZ,)),
                dma((C * D, GX)), dma((C * D, GX)),
                dma((GX * G,)), dma((GX * G,)),
                pltpu.SemaphoreType.REGULAR((max(1, GX - 2),)),
            ],
            compiler_params=pltpu.CompilerParams(
                collective_id=0, has_side_effects=True, vmem_limit_bytes=62 * 1024 * 1024),
        )(snapshot.reshape(S, NI * K, J), factor_two, factor_three).T

    placed = (P(None, "gx", "gz", "gy"), P("gy", None), P("gz", None))
    return jax.shard_map(
        per_device, mesh=mesh, in_specs=placed, out_specs=P("gx", ("gy", "gz")), check_vma=False
    )
```

time: 32.2 us -> 28.7 us (0.89)
  local copies, waits for them, and re-layouts: 3.23 us -> 1.26 us
  Pallas kernels: 28.7 us -> 27.2 us
    pallas_call x1, Pallas kernels: 28.7 us -> 27.2 us  [per_device(): pl.pallas_call(functools.partial(kernel, dims), out_shape=jax.ShapeDtypeS...]
    unnamed x6 -> x1, local copies, waits for them, and re-layouts: 2.58 us -> 1.26 us
    pallas_call x1 -> x0, local copies, waits for them, and re-layouts: 0.65 us -> none  [per_device(): pl.pallas_call(functools.partial(kernel, dims), out_shape=jax.ShapeDtypeS...]
where the time goes in v2:
time: 28.7 us; the launch traced here: 28.5 us
  Pallas kernels  27.2 us (95%)
  local copies, waits for them, and re-layouts  1.26 us (4%)
    pallas_call x1, Pallas kernels, per_device(): pl.pallas_call(functools.partial(kernel, dims), out_shape=jax.ShapeDtypeS...  27.2 us
    unnamed x1, local copies, waits for them, and re-layouts  1.26 us

profile of v2, /device:TPU:0, one launch (start us, length us, event | category | flops | bytes accessed | tf_op | source)
XLA Modules:
  0.0 28.5 jit_solution(8948704527976382916)
XLA Ops:
  0.0 27.2 %shard_map.37 = f32[4,8]{1,0:T(4,128)} custom-call(bf16[16,192,128]{2,1,0:T(8,128)(2,1)} %bitcast.2, bf16[128,128]{1,0:T(8,128)(2,1)} %f2.1, bf16[24,48]{1,0:T(8,128)(2,1)} %f3.1), custom_call_target="tpu_custom_call" | custom-call | tf_op jit(solution)/shard_map/pallas_call | solution.py:175
  27.3 1.3 %copy.5 = f32[8,4]{0,1:T(4,128)} copy(f32[8,4]{0,1:T(4,128)} %bitcast.3) | data formatting | bytes 256

commit v3 on v2

--- a/solution.py
+++ b/solution.py
@@ -63,12 +63,13 @@
         sends.append(remote(f2, f2rx.at[y], sendf2.at[o], recvf2.at[o], {"gy": plus(y, o, GY)}))
     for o in range(1, GZ):
         sends.append(remote(f3own, f3rx.at[z], sendf3.at[o], recvf3.at[o], {"gz": plus(z, o, GZ)}))
-    for t in range(T):
-        for o in range(1, G):
-            p = plus(me, o, G)
-            sends.append(remote(cells(p, t), rx.at[t, me], send1.at[t, o], recv1.at[t, o], plane(p)))
     for copy in sends:
         copy.start()
+    far = sorted(range(GZ), key=lambda b: -min(b, GZ - b))
+    for t in range(T):
+        for a, b in [(a, b) for a in reversed(range(GY)) for b in far if a or b]:
+            p = plus(y, a, GY) * GZ + plus(z, b, GZ)
+            remote(cells(p, t), rx.at[t, me], send1.at[t], recv1.at[t], plane(p)).start()
 
     for step in range(GX - 2):
         neighbours(line.at[step])
@@ -94,9 +95,8 @@
 
     for t in range(T):
         own[t].wait()
-        for o in range(1, G):
-            p = plus(me, G - o, G)
-            remote(cells(me, t), rx.at[t, p], send1.at[t, o], recv1.at[t, o], plane(p)).wait_recv()
+        arrived = rx.at[t, pl.ds(0, G - 1)]
+        remote(arrived, arrived, send1.at[t], recv1.at[t], plane(plus(me, 1, G))).wait_recv()
         second = []
         for b in range(GZ):
             wide = jnp.concatenate([rx[t, a * GZ + b] for a in range(GY)], axis=1)
@@ -117,17 +117,15 @@
             tx2[t, b] = z32[t, b * share:(b + 1) * share, :].astype(jnp.bfloat16)
         for o in range(1, GX):
             q = plus(x, o, GX)
-            copy = remote(tx2.at[t, q], rx2.at[t, x], send2.at[t, o], recv2.at[t, o], {"gx": q})
+            copy = remote(tx2.at[t, q], rx2.at[t, x], send2.at[t], recv2.at[t], {"gx": q})
             copy.start()
-            sends.append(copy)
         rx2[t, x] = tx2[t, x]
 
     gram = None
     for c in range(C):
         for t in range(c * D, c * D + D):
-            for o in range(1, GX):
-                q = plus(x, GX - o, GX)
-                remote(tx2.at[t, q], rx2.at[t, q], send2.at[t, o], recv2.at[t, o], {"gx": q}).wait_recv()
+            gathered = rx2.at[t, pl.ds(0, GX - 1)]
+            remote(gathered, gathered, send2.at[t], recv2.at[t], {"gx": plus(x, 1, GX)}).wait_recv()
         blocks = [rx2[c * D + d, b].astype(jnp.float32) for b in range(GX) for d in range(D)]
         fibres = jnp.concatenate(
             [jnp.concatenate([block[r * NI_:(r + 1) * NI_] for block in blocks], axis=0) for r in range(R3 // GX)],
@@ -141,19 +139,23 @@
     for o in range(1, N):
         d = lax.rem(flat + o, N)
         dx, dp = lax.div(d, G), lax.rem(d, G)
-        copy = remote(g.at[dp], rx4.at[flat], send4.at[o], recv4.at[o], {"gx": dx, **plane(dp)})
+        copy = remote(g.at[dp], rx4.at[flat], send4.at[0], recv4.at[0], {"gx": dx, **plane(dp)})
         copy.start()
-        sends.append(copy)
     rx4[flat] = g[me]
-    for o in range(1, N):
-        d = lax.rem(flat + N - o, N)
-        remote(g.at[0], rx4.at[d], send4.at[o], recv4.at[o], {"gx": lax.div(d, G), **plane(lax.rem(d, G))}).wait_recv()
+    for t in range(T):
+        arrived = rx.at[t, pl.ds(0, G - 1)]
+        remote(arrived, arrived, send1.at[t], recv1.at[t], plane(plus(me, 1, G))).wait_send()
+        gathered = rx2.at[t, pl.ds(0, GX - 1)]
+        remote(gathered, gathered, send2.at[t], recv2.at[t], {"gx": plus(x, 1, GX)}).wait_send()
+    for copy in sends:
+        copy.wait_send()
+    others = rx4.at[pl.ds(0, N - 1)]
+    remote(others, others, send4.at[0], recv4.at[0], plane(plus(me, 1, G))).wait_recv()
     summed = jnp.sum(rx4[...], axis=0)
     lanes = summed.shape[1]
     summed = pltpu.roll(summed, lax.rem(lanes - NI * x, lanes), 1)
     out[...] = summed[:, :NI] / total
-    for copy in sends:
-        copy.wait_send()
+    remote(others, others, send4.at[0], recv4.at[0], plane(plus(me, 1, G))).wait_send()
 
 
 def solution(mesh):
@@ -174,7 +176,7 @@
         f32, bf16 = jnp.float32, jnp.bfloat16
         return pl.pallas_call(
             functools.partial(kernel, dims),
-            out_shape=jax.ShapeDtypeStruct((N1 // G, NI), f32),
+            out_shape=pltpu.VMEM((N1 // G, NI), f32),
             in_specs=[pl.BlockSpec(memory_space=pl.ANY)] * 3,
             out_specs=pl.BlockSpec(memory_space=pltpu.VMEM),
             scratch_shapes=[
@@ -190,11 +192,11 @@
                 pltpu.VMEM((G, N1 // G, lanes), f32),
                 pltpu.VMEM((GX * G, N1 // G, lanes), f32),
                 dma((C * D + 2,)),
-                dma((C * D, G)), dma((C * D, G)),
+                dma((C * D,)), dma((C * D,)),
                 dma((GY,)), dma((GY,)),
                 dma((GZ,)), dma((GZ,)),
-                dma((C * D, GX)), dma((C * D, GX)),
-                dma((GX * G,)), dma((GX * G,)),
+                dma((C * D,)), dma((C * D,)),
+                dma((1,)), dma((1,)),
                 pltpu.SemaphoreType.REGULAR((max(1, GX - 2),)),
             ],
             compiler_params=pltpu.CompilerParams(

time: 28.7 us -> 25.7 us (0.90)
  Pallas kernels: 27.2 us -> 24.9 us
  local copies, waits for them, and re-layouts: 1.26 us -> 0.58 us
    pallas_call x1, Pallas kernels: 27.2 us -> 24.9 us  [per_device(): pl.pallas_call(functools.partial(kernel, dims), out_shape=pltpu.VMEM((N1...]
    unnamed x1, local copies, waits for them, and re-layouts: 1.26 us -> 0.58 us
where the time goes in v3:
time: 25.7 us; the launch traced here: 25.5 us
  Pallas kernels  24.9 us (97%)
  local copies, waits for them, and re-layouts  0.58 us (2%)
    pallas_call x1, Pallas kernels, per_device(): pl.pallas_call(functools.partial(kernel, dims), out_shape=pltpu.VMEM((N1...  24.9 us
    unnamed x1, local copies, waits for them, and re-layouts  0.58 us

profile of v3, /device:TPU:0, one launch (start us, length us, event | category | flops | bytes accessed | tf_op | source)
XLA Modules:
  0.0 25.5 jit_solution(1591994578153347735)
XLA Ops:
  0.0 24.9 %shard_map.37 = f32[4,8]{1,0:T(4,128)S(1)} custom-call(bf16[16,192,128]{2,1,0:T(8,128)(2,1)} %bitcast.3, bf16[128,128]{1,0:T(8,128)(2,1)} %f2.1, bf16[24,48]{1,0:T(8,128)(2,1)} %f3.1), custom_call_target="tpu_custom_call" | custom-call | tf_op jit(solution)/shard_map/pallas_call | solution.py:177
  24.9 0.6 %copy.5 = f32[8,4]{0,1:T(4,128)} copy(f32[8,4]{0,1:T(4,128)S(1)} %bitcast.2) | data formatting | bytes 256

commit v4 on v3

--- a/solution.py
+++ b/solution.py
@@ -33,8 +33,11 @@
             src_ref=src, dst_ref=dst, send_sem=send, recv_sem=recv, device_id=device, device_id_type=MESH)
 
     barrier = pltpu.get_barrier_semaphore()
-    for o in range(1, G):
-        pl.semaphore_signal(barrier, inc=1, device_id=plane(plus(me, o, G)), device_id_type=MESH)
+    for o in range(1, GZ):
+        pl.semaphore_signal(barrier, inc=1, device_id={"gz": plus(z, o, GZ)}, device_id_type=MESH)
+    for o in range(1, GY):
+        pl.semaphore_signal(barrier, inc=1, device_id={"gy": plus(y, o, GY)}, device_id_type=MESH)
+
     def neighbours(semaphore):
         @pl.when(x > 0)
         def _():
@@ -52,24 +55,37 @@
     own.append(pltpu.make_async_copy(f2, f2rx.at[y], local_sem.at[T]))
     for copy in own:
         copy.start()
+    pl.semaphore_wait(barrier, GY - 1 + GZ - 1 + beside)
+
+    far = sorted(range(GZ), key=lambda b: -min(b, GZ - b))
+
+    near = [(0, b) for b in far if b] + [(a, 0) for a in range(1, GY)]
+    cross = [(a, b) for a in reversed(range(1, GY)) for b in far if b]
+
+    def spread(t, offsets):
+        for a, b in offsets:
+            place = {"gy": plus(y, a, GY), "gz": plus(z, b, GZ)}
+            p = place["gy"] * GZ + place["gz"]
+            remote(cells(p, t), rx.at[t, me], send1.at[t], recv1.at[t], place).start()
+
+    for o in range(1, GY):
+        pl.semaphore_signal(line.at[GX - 2], inc=1, device_id={"gy": plus(y, o, GY)}, device_id_type=MESH)
+    spread(0, near)
+    pl.semaphore_wait(line.at[GX - 2], GY - 1)
+    spread(0, cross)
     first.wait()
     f3own[...] = f3raw[...].astype(jnp.float32)
+    sends = []
+    for o in range(1, GZ):
+        sends.append(remote(f3own, f3rx.at[z], sendf3.at[o], recvf3.at[o], {"gz": plus(z, o, GZ)}))
+    for o in range(1, GY):
+        sends.append(remote(f2, f2rx.at[y], sendf2.at[o], recvf2.at[o], {"gy": plus(y, o, GY)}))
+    for copy in sends:
+        copy.start()
+    for t in range(1, T):
+        spread(t, cross + near)
     f3rx[z] = f3own[...]
     g[...] = jnp.zeros_like(g)
-    pl.semaphore_wait(barrier, G - 1 + beside)
-
-    sends = []
-    for o in range(1, GY):
-        sends.append(remote(f2, f2rx.at[y], sendf2.at[o], recvf2.at[o], {"gy": plus(y, o, GY)}))
-    for o in range(1, GZ):
-        sends.append(remote(f3own, f3rx.at[z], sendf3.at[o], recvf3.at[o], {"gz": plus(z, o, GZ)}))
-    for copy in sends:
-        copy.start()
-    far = sorted(range(GZ), key=lambda b: -min(b, GZ - b))
-    for t in range(T):
-        for a, b in [(a, b) for a in reversed(range(GY)) for b in far if a or b]:
-            p = plus(y, a, GY) * GZ + plus(z, b, GZ)
-            remote(cells(p, t), rx.at[t, me], send1.at[t], recv1.at[t], plane(p)).start()
 
     for step in range(GX - 2):
         neighbours(line.at[step])
@@ -136,11 +152,12 @@
     for b in range(G):
         g[b, :, :N1] = gram[b * W:(b + 1) * W]
     flat, N = x * G + me, GX * G
-    for o in range(1, N):
-        d = lax.rem(flat + o, N)
-        dx, dp = lax.div(d, G), lax.rem(d, G)
-        copy = remote(g.at[dp], rx4.at[flat], send4.at[0], recv4.at[0], {"gx": dx, **plane(dp)})
-        copy.start()
+    columns = [plus(me, b, G) for b in range(G)]
+    places = [plane(p) for p in columns]
+    for a in range(GX):
+        dx = plus(x, a, GX)
+        for b in range(1 if a == 0 else 0, G):
+            remote(g.at[columns[b]], rx4.at[flat], send4.at[0], recv4.at[0], {"gx": dx, **places[b]}).start()
     rx4[flat] = g[me]
     for t in range(T):
         arrived = rx.at[t, pl.ds(0, G - 1)]
@@ -197,7 +214,7 @@
                 dma((GZ,)), dma((GZ,)),
                 dma((C * D,)), dma((C * D,)),
                 dma((1,)), dma((1,)),
-                pltpu.SemaphoreType.REGULAR((max(1, GX - 2),)),
+                pltpu.SemaphoreType.REGULAR((GX - 1,)),
             ],
             compiler_params=pltpu.CompilerParams(
                 collective_id=0, has_side_effects=True, vmem_limit_bytes=62 * 1024 * 1024),

time: 25.7 us -> 25.5 us (level)
  no operation moved by 1% of the time
where the time goes in v4:
time: 25.5 us; the launch traced here: 25.4 us
  Pallas kernels  24.8 us (97%)
  local copies, waits for them, and re-layouts  0.58 us (2%)
    pallas_call x1, Pallas kernels, per_device(): pl.pallas_call(functools.partial(kernel, dims), out_shape=pltpu.VMEM((N1...  24.8 us
    unnamed x1, local copies, waits for them, and re-layouts  0.58 us

profile of v4, /device:TPU:0, one launch (start us, length us, event | category | flops | bytes accessed | tf_op | source)
XLA Modules:
  0.0 25.4 jit_solution(1991329086048016438)
XLA Ops:
  0.0 24.8 %shard_map.37 = f32[4,8]{1,0:T(4,128)S(1)} custom-call(bf16[16,192,128]{2,1,0:T(8,128)(2,1)} %bitcast.3, bf16[128,128]{1,0:T(8,128)(2,1)} %f2.1, bf16[24,48]{1,0:T(8,128)(2,1)} %f3.1), custom_call_target="tpu_custom_call" | custom-call | tf_op jit(solution)/shard_map/pallas_call | solution.py:194
  24.8 0.6 %copy.5 = f32[8,4]{0,1:T(4,128)} copy(f32[8,4]{0,1:T(4,128)S(1)} %bitcast.2) | data formatting | bytes 256

commit v5 on v4

--- a/solution.py
+++ b/solution.py
@@ -70,6 +70,9 @@
 
     for o in range(1, GY):
         pl.semaphore_signal(line.at[GX - 2], inc=1, device_id={"gy": plus(y, o, GY)}, device_id_type=MESH)
+    early = [remote(f2, f2rx.at[y], sendf2.at[o], recvf2.at[o], {"gy": plus(y, o, GY)}) for o in range(1, GY)]
+    for copy in early:
+        copy.start()
     spread(0, near)
     pl.semaphore_wait(line.at[GX - 2], GY - 1)
     spread(0, cross)
@@ -78,10 +81,9 @@
     sends = []
     for o in range(1, GZ):
         sends.append(remote(f3own, f3rx.at[z], sendf3.at[o], recvf3.at[o], {"gz": plus(z, o, GZ)}))
-    for o in range(1, GY):
-        sends.append(remote(f2, f2rx.at[y], sendf2.at[o], recvf2.at[o], {"gy": plus(y, o, GY)}))
     for copy in sends:
         copy.start()
+    sends.extend(early)
     for t in range(1, T):
         spread(t, cross + near)
     f3rx[z] = f3own[...]

time: 25.5 us -> 25.2 us (0.988)
  Pallas kernels: 24.8 us -> 24.4 us
    pallas_call x1, Pallas kernels: 24.8 us -> 24.4 us  [per_device(): pl.pallas_call(functools.partial(kernel, dims), out_shape=pltpu.VMEM((N1...]
where the time goes in v5:
time: 25.2 us; the launch traced here: 25 us
  Pallas kernels  24.4 us (97%)
  local copies, waits for them, and re-layouts  0.58 us (2%)
    pallas_call x1, Pallas kernels, per_device(): pl.pallas_call(functools.partial(kernel, dims), out_shape=pltpu.VMEM((N1...  24.4 us
    unnamed x1, local copies, waits for them, and re-layouts  0.58 us

profile of v5, /device:TPU:0, one launch (start us, length us, event | category | flops | bytes accessed | tf_op | source)
XLA Modules:
  0.0 25.0 jit_solution(12452600151830047752)
XLA Ops:
  0.0 24.4 %shard_map.37 = f32[4,8]{1,0:T(4,128)S(1)} custom-call(bf16[16,192,128]{2,1,0:T(8,128)(2,1)} %bitcast.3, bf16[128,128]{1,0:T(8,128)(2,1)} %f2.1, bf16[24,48]{1,0:T(8,128)(2,1)} %f3.1), custom_call_target="tpu_custom_call" | custom-call | tf_op jit(solution)/shard_map/pallas_call | solution.py:196
  24.4 0.6 %copy.5 = f32[8,4]{0,1:T(4,128)} copy(f32[8,4]{0,1:T(4,128)S(1)} %bitcast.2) | data formatting | bytes 256

commit v6 on v5

--- a/solution.py
+++ b/solution.py
@@ -12,7 +12,7 @@
 
 
 def kernel(dims, snap, f2, f3, out, rx, f2rx, f3raw, f3own, f3rx, mix, z32, tx2, rx2, g, rx4,
-           local_sem, send1, recv1, sendf2, recvf2, sendf3, recvf3, send2, recv2, send4, recv4, line):
+           local_sem, send1, recv1, sendf2, recvf2, sendf3, recvf3, send2, recv2, send4, recv4, line, spread2):
     GX, GY, GZ, S, C, D, H, NI, K, R3, N1, total = dims
     G = GY * GZ
     T, NI_, W = C * D, NI // D, N1 // G
@@ -70,7 +70,10 @@
 
     for o in range(1, GY):
         pl.semaphore_signal(line.at[GX - 2], inc=1, device_id={"gy": plus(y, o, GY)}, device_id_type=MESH)
-    early = [remote(f2, f2rx.at[y], sendf2.at[o], recvf2.at[o], {"gy": plus(y, o, GY)}) for o in range(1, GY)]
+    J = f2.shape[0]
+    Q = GX if J % (16 * GX) == 0 else 1
+    mine = pl.ds(pl.multiple_of(x * (J // Q), J // Q), J // Q) if Q > 1 else pl.ds(0, J)
+    early = [remote(f2.at[mine], f2rx.at[y, mine], sendf2.at[o], recvf2.at[o], {"gy": plus(y, o, GY)}) for o in range(1, GY)]
     for copy in early:
         copy.start()
     spread(0, near)
@@ -95,7 +98,13 @@
 
     for o in range(1, GY):
         q = plus(y, GY - o, GY)
-        remote(f2, f2rx.at[q], sendf2.at[o], recvf2.at[o], {"gy": q}).wait_recv()
+        remote(f2.at[mine], f2rx.at[q, mine], sendf2.at[o], recvf2.at[o], {"gy": q}).wait_recv()
+        for b in range(1, GX if Q > 1 else 1):
+            copy = remote(f2rx.at[q, mine], f2rx.at[q, mine], spread2.at[o], spread2.at[GY + o], {"gx": plus(x, b, GX)})
+            copy.start()
+    for o in range(1, GY if Q > 1 else 1):
+        rest = f2rx.at[plus(y, GY - o, GY), pl.ds(0, (GX - 1) * (J // Q))]
+        remote(rest, rest, spread2.at[o], spread2.at[GY + o], {"gx": plus(x, 1, GX)}).wait_recv()
     own[T].wait()
     for o in range(1, GZ):
         q = plus(z, GZ - o, GZ)
@@ -168,6 +177,9 @@
         remote(gathered, gathered, send2.at[t], recv2.at[t], {"gx": plus(x, 1, GX)}).wait_send()
     for copy in sends:
         copy.wait_send()
+    for o in range(1, GY if Q > 1 else 1):
+        rest = f2rx.at[plus(y, GY - o, GY), pl.ds(0, (GX - 1) * (J // Q))]
+        remote(rest, rest, spread2.at[o], spread2.at[GY + o], {"gx": plus(x, 1, GX)}).wait_send()
     others = rx4.at[pl.ds(0, N - 1)]
     remote(others, others, send4.at[0], recv4.at[0], plane(plus(me, 1, G))).wait_recv()
     summed = jnp.sum(rx4[...], axis=0)
@@ -217,6 +229,7 @@
                 dma((C * D,)), dma((C * D,)),
                 dma((1,)), dma((1,)),
                 pltpu.SemaphoreType.REGULAR((GX - 1,)),
+                dma((2 * GY,)),
             ],
             compiler_params=pltpu.CompilerParams(
                 collective_id=0, has_side_effects=True, vmem_limit_bytes=62 * 1024 * 1024),

time: 25.2 us -> 25 us (level)
  no operation moved by 1% of the time
where the time goes in v6:
time: 25 us; the launch traced here: 24.9 us
  Pallas kernels  24.3 us (97%)
  local copies, waits for them, and re-layouts  0.58 us (2%)
    pallas_call x1, Pallas kernels, per_device(): pl.pallas_call(functools.partial(kernel, dims), out_shape=pltpu.VMEM((N1...  24.3 us
    unnamed x1, local copies, waits for them, and re-layouts  0.58 us

profile of v6, /device:TPU:0, one launch (start us, length us, event | category | flops | bytes accessed | tf_op | source)
XLA Modules:
  0.0 24.9 jit_solution(9282814705482565667)
XLA Ops:
  0.0 24.3 %shard_map.37 = f32[4,8]{1,0:T(4,128)S(1)} custom-call(bf16[16,192,128]{2,1,0:T(8,128)(2,1)} %bitcast.3, bf16[128,128]{1,0:T(8,128)(2,1)} %f2.1, bf16[24,48]{1,0:T(8,128)(2,1)} %f3.1), custom_call_target="tpu_custom_call" | custom-call | tf_op jit(solution)/shard_map/pallas_call | solution.py:208
  24.3 0.6 %copy.5 = f32[8,4]{0,1:T(4,128)} copy(f32[8,4]{0,1:T(4,128)S(1)} %bitcast.2) | data formatting | bytes 256
